TPU v7x, 128 devices: a whole 4x4x4 slice. The times are simulated.
128 devices in a mesh: aa: 16 (over x_hi, z, core), ba: 8 (over y, x_lo).
Axes of the slice: x: 4 (x_hi: 2, x_lo: 2; x = x_hi * 2 + x_lo), y: 4, z: 4, core: 2. Of those that a mesh axis runs over, the one named last changes fastest.
Arguments:
- field: bfloat16 [1024, 1024, 1024], P(None, 'aa', 'ba'), may hold values from -8 to 8
- mode_one: bfloat16 [1024, 256], replicated, may hold values from -0.1875 to 0.1875
- mode_two: bfloat16 [1024, 256], P('aa'), may hold values from -0.1875 to 0.1875
Outputs:
- gram: float32 [1024, 1024], P('ba')
All inputs are finite; a program needn't handle non-finite values.
Results may differ from a plain program's by a relative error of at most 0.00077.
Values may be sent and summed in bfloat16 or wider, within the bound.
A program may use at most 192 MiB of HBM per device.

v0:
```python
import functools

import jax
import jax.numpy as jnp
from jax import lax
from jax.experimental import pallas as pl
from jax.experimental.pallas import tpu as pltpu
from jax.sharding import PartitionSpec as P

BF, F32 = jnp.bfloat16, jnp.float32
MESH = pl.DeviceIdType.MESH
JT = 16
CLASSES = (((0, 1), (2, 3), (4,)), ((2, 3), (0,), (1,)))
START = ((0, 1, 2), (2, 0, 1))
ROOM = (2, 2, 1)


def where_am_i():
    aa, ba = lax.axis_index("aa"), lax.axis_index("ba")
    core, z = lax.rem(aa, 2), lax.rem(lax.div(aa, 2), 4)
    x = 2 * lax.div(aa, 8) + lax.rem(ba, 2)
    y = lax.div(ba, 2)
    return aa, ba, x, y, z, core


def place(x, y, z, core):
    aa = 8 * lax.div(x, 2) + 2 * z + core
    ba = 2 * y + lax.rem(x, 2)
    return aa, ba


def total_wait(ref, sem):
    pltpu.make_async_copy(ref, ref, sem).wait()


def kernel(
    field, m1_hbm, m2_hbm, out,
    fbuf, wide, obuf, sbuf, rbuf, m1, m1t, m2, m2buf, m2t, cacc, cc, left, acc, blocks,
    fsem, wsem, send, recv, m2send, m2recv, m2sem, csend, crecv, gsend, grecv, osend, brecv, wsend, wrecv, *parts,
):
    gs, r1, s1, r2, s2, r3 = (parts[3 * n : 3 * n + 3] for n in range(6))
    aa, ba, x, y, z, core = where_am_i()
    tiles = fbuf.shape[0]
    me = 8 * aa + ba
    sibling = {"aa": aa + 1 - 2 * core, "ba": ba}
    place_in_k = 8 * core + 4 * lax.div(x, 2) + z

    def load(tile, part):
        rows = pl.ds(256 * part, 256)
        return pltpu.make_async_copy(
            field.at[rows, pl.ds(JT * tile, JT), :], fbuf.at[tile, rows], fsem.at[tile, part]
        )

    barrier = pltpu.get_barrier_semaphore()

    def greet(aa_mask, ba_mask):
        pl.semaphore_signal(
            barrier, inc=1, device_id={"aa": aa ^ aa_mask, "ba": ba ^ ba_mask}, device_id_type=MESH
        )

    for ba_mask in range(1, 8):
        greet(0, ba_mask)

    @pl.loop(1, 16)
    def _(aa_mask):
        for ba_mask in range(8):
            greet(aa_mask, ba_mask)

    load_m1 = pltpu.make_async_copy(m1_hbm, m1, wsem.at[0])
    load_m2 = pltpu.make_async_copy(m2_hbm, m2, wsem.at[1])
    load_m1.start()
    for part in range(4):
        load(0, part).start()
    load_m2.start()

    for tile in range(1, tiles):
        for part in range(4):
            load(tile, part).start()

    load_m1.wait()
    m1t[...] = m1[...].T

    def send_rows(tile, first, count, sem):
        rows = pl.ds(pl.multiple_of(JT * place_in_k, JT), JT)

        def block(to):
            mine = sbuf.at[tile, pl.ds(2 * to + first, count)]
            return mine, rbuf.at[tile, pl.ds(first, count), ba, rows, :]

        def start(step):
            to = me ^ ((37 * step) & 127)
            mine, there = block(to)
            pltpu.make_async_remote_copy(
                mine, there, send, sem, device_id={"aa": to >> 3, "ba": to & 7}, device_id_type=MESH
            ).start()

        for step in range(1, 8):
            start(step)
        pl.loop(1, 16)(lambda turn: [start(8 * turn + step) for step in range(8)] and None)

        mine, there = block(me)
        pltpu.make_async_copy(mine, there, sem).start()

    @pl.loop(0, tiles)
    def _(tile):
        @pl.loop(0, 4)
        def _(part):
            load(tile, part).wait()

            @pl.loop(0, 32, unroll=4)
            def _(group):
                at = 256 * part + 8 * group
                wide[pl.ds(pl.multiple_of(JT * at, 128), 128), :] = (
                    fbuf[tile, pl.ds(at, 8)].reshape(128, 128).astype(F32)
                )

        @pl.loop(0, JT // 2)
        def _(pair):
            both = jnp.concatenate(
                [wide[pl.ds(2 * pair + n, 1024, stride=JT), :] for n in range(2)], axis=1
            ).astype(BF)
            got = jnp.dot(m1t[...], both, preferred_element_type=F32)
            for n in range(2):
                obuf[pl.ds(pl.multiple_of(512 * pair + 256 * n, 256), 256), :] = got[:, 128 * n : 128 * n + 128]

        @pl.loop(0, 256, unroll=8)
        def _(r):
            sbuf[tile, r] = obuf[pl.ds(r, JT, stride=256), :].astype(BF)

        @pl.when(tile == 0)
        def _():
            pl.semaphore_wait(barrier, 127)

        @pl.when(tile < 3)
        def _():
            send_rows(tile, 0, 2, recv.at[tile])

        @pl.when(tile == 3)
        def _():
            for half in range(2):
                send_rows(tile, half, 1, recv.at[3 + half])

        @pl.when(tile == 1)
        def _():
            load_m2.wait()
            mine = m2buf.at[:, place_in_k]
            for mask in range(1, 8):
                to_aa, to_ba = place(x ^ (2 * (mask // 4)), y, z ^ (mask % 4), core)
                pltpu.make_async_remote_copy(
                    m2, mine, m2send, m2recv, device_id={"aa": to_aa, "ba": to_ba}, device_id_type=MESH
                ).start()
            pltpu.make_async_copy(m2, mine, m2recv).start()

    half_of_m2 = m2buf.at[:, pl.ds(8 * core, 8)]
    total_wait(half_of_m2, m2recv)
    pass_m2 = pltpu.make_async_remote_copy(
        half_of_m2, half_of_m2, m2sem.at[0], m2sem.at[1], device_id=sibling, device_id_type=MESH
    )
    pass_m2.start()
    pass_m2.wait()
    for tile in range(4):
        m2t[tile] = m2buf[tile].reshape(256, 256).T

    def share(half, pair):
        blocks = pl.ds(2 * pair, 2)
        return pltpu.make_async_remote_copy(
            cc.at[blocks, pl.ds(256 * half, 256), :], cc.at[blocks, pl.ds(512 + 256 * half, 256), :],
            csend.at[half, pair], crecv.at[half, pair], device_id=sibling, device_id_type=MESH,
        )

    for tile in range(4):
        if tile < 3:
            total_wait(rbuf.at[tile], recv.at[tile])
        for half in range(2):
            if tile == 3:
                total_wait(rbuf.at[tile, half], recv.at[3 + half])

            @pl.loop(0, 4, unroll=2)
            def _(pair):
                both = jnp.concatenate([rbuf[tile, half, 2 * pair], rbuf[tile, half, 2 * pair + 1]], axis=1)
                got = jnp.dot(m2t[tile], both, preferred_element_type=F32)
                if tile > 0:
                    got += cacc[half, pair]
                if tile < 3:
                    cacc[half, pair] = got
                else:
                    cc[2 * pair, pl.ds(256 * half, 256), :] = got[:, :128].astype(BF)
                    cc[2 * pair + 1, pl.ds(256 * half, 256), :] = got[:, 128:].astype(BF)
                    share(half, pair).start()

    where = (x, y, z)
    sums, got_from = (gs, s1, s2), (r1, r2, r3)
    own_k, their_k = pl.ds(0, 512), pl.ds(512, 512)
    rows = [(low_y, low_x) for low_y in range(2) for low_x in range(2)]

    def row_of(low_y, low_x):
        return 4 * core + 2 * low_y + low_x

    def on_core(which):
        return lambda body: pl.when(core == which)(lambda: body(which))

    def term(rows_of_k, left, block_row, columns):
        right = jnp.concatenate([cc[lax.rem(block_row + d, 8), rows_of_k, :] for d in columns], axis=1)
        return jnp.dot(left, right, preferred_element_type=F32)

    def pieces(which, got, low_y, low_x, k):
        for octet in range(16):
            owner = (2 * (octet >> 3) + low_x, 2 * (octet & 1) + low_y, (octet >> 1) & 3)
            index = tuple(owner[(START[which][k] + stage) % 3] for stage in range(3))
            for n in range(len(CLASSES[which][k])):
                yield gs[k], index + (n,), got[8 * octet : 8 * octet + 8, 128 * n : 128 * n + 128]

    def filled(which, ref, k):
        before = (slice(None),) * (len(ref.shape) - 3)
        return ref.at[before + (pl.ds(0, len(CLASSES[which][k])),)]

    def own_part(which):
        columns = sum(sorted(CLASSES[which]), ())
        for low_y, low_x in rows:
            block_row = row_of(low_y, low_x)
            got = term(own_k, cc[block_row, own_k, :].T, block_row, columns)
            for k, mine in enumerate(CLASSES[which]):
                part = got[:, 128 * mine[0] : 128 * mine[-1] + 128]
                for ref, index, value in pieces(which, part, low_y, low_x, k):
                    ref[index] = value

    def scatter(which, k, stage):
        axis = (START[which][k] + stage) % 3
        for mask in range(1, 4):
            there = [x, y, z]
            there[axis] = there[axis] ^ mask
            to_aa, to_ba = place(*there, core)
            pltpu.make_async_remote_copy(
                filled(which, sums[stage][k], k).at[where[axis] ^ mask],
                filled(which, got_from[stage][k], k).at[mask - 1], gsend, grecv.at[k, stage],
                device_id={"aa": to_aa, "ba": to_ba}, device_id_type=MESH,
            ).start()

    def gathered(which, k, stage):
        total_wait(filled(which, got_from[stage][k], k), grecv.at[k, stage])
        got = filled(which, got_from[stage][k], k)
        own = filled(which, sums[stage][k], k)[where[(START[which][k] + stage) % 3]]
        return own + got[0] + got[1] + got[2]

    def sum_up(which):
        for k, columns in enumerate(CLASSES[which]):
            for low_y, low_x in rows:
                got = term(their_k, left[2 * low_y + low_x], row_of(low_y, low_x), columns)
                for ref, index, value in pieces(which, got, low_y, low_x, k):
                    ref[index] += value
            scatter(which, k, 0)
        for stage in range(2):
            for k in range(3):
                filled(which, sums[stage + 1][k], k)[...] = gathered(which, k, stage)
                scatter(which, k, stage + 1)
        for k, columns in enumerate(CLASSES[which]):
            acc[pl.ds(columns[0], len(columns))] = gathered(which, k, 2) * (1.0 / 65536.0)

    mine = 4 * core + 2 * lax.rem(y, 2) + lax.rem(x, 2)
    taker = lax.div(x, 2)
    own = pl.ds(pl.multiple_of(8 * (8 * taker + 2 * z + lax.div(y, 2)), 8), 8)
    inside = jnp.logical_and(mine == ba, taker == core)
    across = jnp.logical_and(mine + 4 == ba, taker == core)

    def spread(which):
        count = 5 - which

        @pl.loop(0, 8)
        def _(step):
            to_aa = (aa ^ (2 * step) ^ core) | taker
            self = jnp.logical_and(inside, step == 0)
            source, target = acc.at[pl.ds(0, count)], blocks.at[pl.ds(0, count), own, :]

            @pl.when(self)
            def _():
                pltpu.make_async_copy(source, target, brecv).start()

            @pl.when(jnp.logical_not(self))
            def _():
                pltpu.make_async_remote_copy(
                    source, target, osend, brecv, device_id={"aa": to_aa, "ba": mine}, device_id_type=MESH
                ).start()

            for d in range(1, 4):
                pltpu.make_async_remote_copy(
                    acc.at[d], blocks.at[4 + d, own, :], osend, brecv,
                    device_id={"aa": to_aa, "ba": lax.rem(mine + d, 8)}, device_id_type=MESH,
                ).start()

            if which == 0:
                self = jnp.logical_and(across, step == 0)

                @pl.when(self)
                def _():
                    pltpu.make_async_copy(acc.at[4], blocks.at[4, own, :], brecv).start()

                @pl.when(jnp.logical_not(self))
                def _():
                    pltpu.make_async_remote_copy(
                        acc.at[4], blocks.at[4, own, :], osend, brecv,
                        device_id={"aa": to_aa, "ba": mine + 4}, device_id_type=MESH,
                    ).start()

    for which in range(2):
        on_core(which)(own_part)
    for half in range(2):
        for pair in range(4):
            share(half, pair).wait()
    for low_y, low_x in rows:
        left[2 * low_y + low_x] = cc[row_of(low_y, low_x), their_k, :].T
    for which in range(2):
        on_core(which)(sum_up)
    for which in range(2):
        on_core(which)(spread)

    half = blocks.at[:, pl.ds(pl.multiple_of(64 * core, 64), 64), :]
    total_wait(half, brecv)
    swap = pltpu.make_async_remote_copy(
        half, half, wsend, wrecv, device_id=sibling, device_id_type=MESH
    )
    swap.start()
    swap.wait()

    def put(d, value):
        out[:, pl.ds(pl.multiple_of(128 * lax.rem(ba + d, 8), 128), 128)] = value

    for d in range(4):
        put(d, blocks[d])
    for d in range(1, 4):
        put(8 - d, blocks[4 + d].T)

    @pl.when(ba < 4)
    def _():
        put(4, blocks[4])

    @pl.when(ba >= 4)
    def _():
        put(4, blocks[4].T)

    total_wait(sbuf.at[:, pl.ds(0, 254)], send)
    total_wait(m2buf.at[:, pl.ds(0, 7)], m2send)

    def sent(which):
        for stage in range(3):
            for k in range(3):
                total_wait(filled(which, got_from[stage][k], k), gsend)
        count = 5 - which
        total_wait(blocks.at[pl.ds(0, 3), pl.ds(0, 64), :], osend)
        total_wait(blocks.at[pl.ds(0, count), pl.ds(0, 56), :], osend)

        @pl.when(jnp.logical_not(inside))
        def _():
            total_wait(blocks.at[pl.ds(0, count), pl.ds(0, 8), :], osend)

        if which == 0:
            total_wait(blocks.at[pl.ds(0, 1), pl.ds(0, 56), :], osend)

            @pl.when(jnp.logical_not(across))
            def _():
                total_wait(blocks.at[pl.ds(0, 1), pl.ds(0, 8), :], osend)

    for which in range(2):
        on_core(which)(sent)


def shards(field, mode_one, mode_two):
    dma = pltpu.SemaphoreType.DMA
    hbm = pl.BlockSpec(memory_space=pltpu.HBM)
    return pl.pallas_call(
        kernel,
        out_shape=jax.ShapeDtypeStruct((128, 1024), F32),
        in_specs=[hbm, hbm, hbm],
        out_specs=pl.BlockSpec(memory_space=pltpu.VMEM),
        scratch_shapes=[
            pltpu.VMEM((4, 1024, JT, 128), BF),
            pltpu.VMEM((1024 * JT, 128), F32),
            pltpu.VMEM((JT * 256, 128), F32),
            pltpu.VMEM((4, 256, JT, 128), BF),
            pltpu.VMEM((4, 2, 8, 256, 128), BF),
            pltpu.VMEM((1024, 256), BF),
            pltpu.VMEM((256, 1024), BF),
            pltpu.VMEM((4, JT, 256), BF),
            pltpu.VMEM((4, 16, JT, 256), BF),
            pltpu.VMEM((4, 256, 256), BF),
            pltpu.VMEM((2, 4, 256, 256), F32),
            pltpu.VMEM((8, 1024, 128), BF),
            pltpu.VMEM((4, 128, 512), BF),
            pltpu.VMEM((5, 8, 128), F32),
            pltpu.VMEM((8, 128, 128), F32),
            dma((4, 4)), dma((2,)),
            dma, dma((5,)), dma, dma, dma((2,)),
            dma((2, 4)), dma((2, 4)),
            dma, dma((3, 3)), dma, dma, dma, dma,
            *[
                pltpu.VMEM(shape + (room, 8, 128), F32)
                for shape in ((4, 4, 4), (3, 4, 4), (4, 4), (3, 4), (4,), (3,))
                for room in ROOM
            ],
        ],
        compiler_params=pltpu.CompilerParams(
            collective_id=0, has_side_effects=True, vmem_limit_bytes=53 * 1024 * 1024
        ),
        cost_estimate=pl.CostEstimate(flops=13_000_000_000, bytes_accessed=18_000_000, transcendentals=0),
    )(field, mode_one, mode_two.reshape(4, JT, 256))


def solution(mesh):
    in_specs = (P(None, "aa", "ba"), P(), P("aa", None))
    return jax.shard_map(shards, mesh=mesh, in_specs=in_specs, out_specs=P("ba", None), check_vma=False)
```

profile of v0, /device:TPU:1, one launch (start us, length us, event | category | flops | bytes accessed | tf_op | source)
XLA Modules:
  0.0 95.7 jit_solution(12697942547453396292)
XLA Ops:
  0.0 0.0 copy-start
  0.0 0.8 copy-done
  0.8 94.1 %shard_map.37 = f32[128,1024]{1,0:T(8,128)S(1)} custom-call(bf16[1024,64,128]{2,1,0:T(8,128)(2,1)} %field.1, bf16[1024,256]{1,0:T(8,128)(2,1)} %m1_hbm.1, bf16[4,16,256]{2,1,0:T(8,128)(2,1)S(1)} %bitcast.1), custom_call_target="tpu_custom_call" | custom-call | flops 12999999488 | bytes 18000000 | tf_op jit(solution)/shard_map/pallas_call | solution.py:369
  94.9 0.8 copy.5
Async XLA Ops:
  0.0 0.8 copy-start
where the time goes:
time: 95.9 us; the launch traced here: 95.7 us
  Pallas kernels  94.1 us (98%)
  local copies, waits for them, and re-layouts  1.55 us (2%)
    pallas_call x1, Pallas kernels, shards(): pl.pallas_call(kernel, out_shape=jax.ShapeDtypeStruct((128, 1024), F32),...  94.1 us

commit v1 on v0

--- a/solution.py
+++ b/solution.py
@@ -29,6 +29,12 @@
     return aa, ba
 
 
+def masks(step):
+    one = step ^ (step >> 2)
+    mx, my, mz, mc = (one ^ (step >> 4)) & 3, one & 3, step & 3, (step ^ (step >> 6)) & 1
+    return ((mx >> 1) << 3) | (mz << 1) | mc, (my << 1) | (mx & 1)
+
+
 def total_wait(ref, sem):
     pltpu.make_async_copy(ref, ref, sem).wait()
 
@@ -36,7 +42,7 @@
 def kernel(
     field, m1_hbm, m2_hbm, out,
     fbuf, wide, obuf, sbuf, rbuf, m1, m1t, m2, m2buf, m2t, cacc, cc, left, acc, blocks,
-    fsem, wsem, send, recv, m2send, m2recv, m2sem, csend, crecv, gsend, grecv, osend, brecv, wsend, wrecv, *parts,
+    fsem, wsem, send, recv, m2send, m2recv, m2sem, m2ysend, m2yrecv, csend, crecv, gsend, grecv, osend, brecv, wsend, wrecv, *parts,
 ):
     gs, r1, s1, r2, s2, r3 = (parts[3 * n : 3 * n + 3] for n in range(6))
     aa, ba, x, y, z, core = where_am_i()
@@ -88,7 +94,8 @@
             return mine, rbuf.at[tile, pl.ds(first, count), ba, rows, :]
 
         def start(step):
-            to = me ^ ((37 * step) & 127)
+            aa_mask, ba_mask = masks(step)
+            to = me ^ ((aa_mask << 3) | ba_mask)
             mine, there = block(to)
             pltpu.make_async_remote_copy(
                 mine, there, send, sem, device_id={"aa": to >> 3, "ba": to & 7}, device_id_type=MESH
@@ -100,6 +107,16 @@
 
         mine, there = block(me)
         pltpu.make_async_copy(mine, there, sem).start()
+
+    parity = lax.rem(y, 2)
+
+    def trade_m2(n):
+        gathered = m2buf.at[parity + 2 * n, pl.ds(8 * core, 8)]
+        to_aa, to_ba = place(x, y ^ (1 + 2 * n), z, core)
+        return pltpu.make_async_remote_copy(
+            gathered, gathered, m2ysend.at[n], m2yrecv.at[n],
+            device_id={"aa": to_aa, "ba": to_ba}, device_id_type=MESH,
+        )
 
     @pl.loop(0, tiles)
     def _(tile):
@@ -140,19 +157,30 @@
             for half in range(2):
                 send_rows(tile, half, 1, recv.at[3 + half])
 
-        @pl.when(tile == 1)
+        @pl.when(tile == 0)
         def _():
             load_m2.wait()
-            mine = m2buf.at[:, place_in_k]
             for mask in range(1, 8):
                 to_aa, to_ba = place(x ^ (2 * (mask // 4)), y, z ^ (mask % 4), core)
-                pltpu.make_async_remote_copy(
-                    m2, mine, m2send, m2recv, device_id={"aa": to_aa, "ba": to_ba}, device_id_type=MESH
+                for n in range(2):
+                    pltpu.make_async_remote_copy(
+                        m2.at[parity + 2 * n], m2buf.at[parity + 2 * n, place_in_k], m2send, m2recv,
+                        device_id={"aa": to_aa, "ba": to_ba}, device_id_type=MESH,
+                    ).start()
+            for n in range(2):
+                pltpu.make_async_copy(
+                    m2.at[parity + 2 * n], m2buf.at[parity + 2 * n, place_in_k], m2recv
                 ).start()
-            pltpu.make_async_copy(m2, mine, m2recv).start()
-
+
+        @pl.when(tile == 2)
+        def _():
+            total_wait(m2buf.at[pl.ds(0, 2), pl.ds(0, 8)], m2recv)
+            for n in range(2):
+                trade_m2(n).start()
+
+    for n in range(2):
+        trade_m2(n).wait()
     half_of_m2 = m2buf.at[:, pl.ds(8 * core, 8)]
-    total_wait(half_of_m2, m2recv)
     pass_m2 = pltpu.make_async_remote_copy(
         half_of_m2, half_of_m2, m2sem.at[0], m2sem.at[1], device_id=sibling, device_id_type=MESH
     )
@@ -338,7 +366,7 @@
         put(4, blocks[4].T)
 
     total_wait(sbuf.at[:, pl.ds(0, 254)], send)
-    total_wait(m2buf.at[:, pl.ds(0, 7)], m2send)
+    total_wait(m2buf.at[pl.ds(0, 2), pl.ds(0, 7)], m2send)
 
     def sent(which):
         for stage in range(3):
@@ -388,7 +416,7 @@
             pltpu.VMEM((5, 8, 128), F32),
             pltpu.VMEM((8, 128, 128), F32),
             dma((4, 4)), dma((2,)),
-            dma, dma((5,)), dma, dma, dma((2,)),
+            dma, dma((5,)), dma, dma, dma((2,)), dma((2,)), dma((2,)),
             dma((2, 4)), dma((2, 4)),
             dma, dma((3, 3)), dma, dma, dma, dma,
             *[

time: 95.9 us -> 93.6 us (0.976)
  Pallas kernels: 94.1 us -> 91.9 us
    pallas_call x1, Pallas kernels: 94.1 us -> 91.9 us  [shards(): pl.pallas_call(kernel, out_shape=jax.ShapeDtypeStruct((128, 1024), F32),...]
where the time goes in v1:
time: 93.6 us; the launch traced here: 93.5 us
  Pallas kernels  91.9 us (98%)
  local copies, waits for them, and re-layouts  1.55 us (2%)
    pallas_call x1, Pallas kernels, shards(): pl.pallas_call(kernel, out_shape=jax.ShapeDtypeStruct((128, 1024), F32),...  91.9 us

profile of v1, /device:TPU:1, one launch (start us, length us, event | category | flops | bytes accessed | tf_op | source)
XLA Modules:
  0.0 93.5 jit_solution(7156471870698050961)
XLA Ops:
  0.0 0.0 copy-start
  0.0 0.8 copy-done
  0.8 91.9 %shard_map.37 = f32[128,1024]{1,0:T(8,128)S(1)} custom-call(bf16[1024,64,128]{2,1,0:T(8,128)(2,1)} %field.1, bf16[1024,256]{1,0:T(8,128)(2,1)} %m1_hbm.1, bf16[4,16,256]{2,1,0:T(8,128)(2,1)S(1)} %bitcast.1), custom_call_target="tpu_custom_call" | custom-call | flops 12999999488 | bytes 18000000 | tf_op jit(solution)/shard_map/pallas_call | solution.py:397
  92.7 0.8 copy.5
Async XLA Ops:
  0.0 0.8 copy-start

commit v2 on v1

--- a/solution.py
+++ b/solution.py
@@ -218,7 +218,7 @@
 
     where = (x, y, z)
     sums, got_from = (gs, s1, s2), (r1, r2, r3)
-    own_k, their_k = pl.ds(0, 512), pl.ds(512, 512)
+    early_k, late_k = pl.ds(0, 768), pl.ds(768, 256)
     rows = [(low_y, low_x) for low_y in range(2) for low_x in range(2)]
 
     def row_of(low_y, low_x):
@@ -246,7 +246,7 @@
         columns = sum(sorted(CLASSES[which]), ())
         for low_y, low_x in rows:
             block_row = row_of(low_y, low_x)
-            got = term(own_k, cc[block_row, own_k, :].T, block_row, columns)
+            got = term(early_k, cc[block_row, early_k, :].T, block_row, columns)
             for k, mine in enumerate(CLASSES[which]):
                 part = got[:, 128 * mine[0] : 128 * mine[-1] + 128]
                 for ref, index, value in pieces(which, part, low_y, low_x, k):
@@ -273,7 +273,7 @@
     def sum_up(which):
         for k, columns in enumerate(CLASSES[which]):
             for low_y, low_x in rows:
-                got = term(their_k, left[2 * low_y + low_x], row_of(low_y, low_x), columns)
+                got = term(late_k, left[2 * low_y + low_x], row_of(low_y, low_x), columns)
                 for ref, index, value in pieces(which, got, low_y, low_x, k):
                     ref[index] += value
             scatter(which, k, 0)
@@ -329,13 +329,14 @@
                         device_id={"aa": to_aa, "ba": mine + 4}, device_id_type=MESH,
                     ).start()
 
+    for pair in range(4):
+        share(0, pair).wait()
     for which in range(2):
         on_core(which)(own_part)
-    for half in range(2):
-        for pair in range(4):
-            share(half, pair).wait()
+    for pair in range(4):
+        share(1, pair).wait()
     for low_y, low_x in rows:
-        left[2 * low_y + low_x] = cc[row_of(low_y, low_x), their_k, :].T
+        left[2 * low_y + low_x] = cc[row_of(low_y, low_x), late_k, :].T
     for which in range(2):
         on_core(which)(sum_up)
     for which in range(2):
@@ -412,7 +413,7 @@
             pltpu.VMEM((4, 256, 256), BF),
             pltpu.VMEM((2, 4, 256, 256), F32),
             pltpu.VMEM((8, 1024, 128), BF),
-            pltpu.VMEM((4, 128, 512), BF),
+            pltpu.VMEM((4, 128, 256), BF),
             pltpu.VMEM((5, 8, 128), F32),
             pltpu.VMEM((8, 128, 128), F32),
             dma((4, 4)), dma((2,)),

time: 93.6 us -> 93.4 us (level)
  no operation moved by 1% of the time
where the time goes in v2:
time: 93.4 us; the launch traced here: 93.2 us
  Pallas kernels  91.6 us (98%)
  local copies, waits for them, and re-layouts  1.55 us (2%)
    pallas_call x1, Pallas kernels, shards(): pl.pallas_call(kernel, out_shape=jax.ShapeDtypeStruct((128, 1024), F32),...  91.6 us

profile of v2, /device:TPU:1, one launch (start us, length us, event | category | flops | bytes accessed | tf_op | source)
XLA Modules:
  0.0 93.2 jit_solution(15887226351703131944)
XLA Ops:
  0.0 0.0 copy-start
  0.0 0.8 copy-done
  0.8 91.6 %shard_map.37 = f32[128,1024]{1,0:T(8,128)S(1)} custom-call(bf16[1024,64,128]{2,1,0:T(8,128)(2,1)} %field.1, bf16[1024,256]{1,0:T(8,128)(2,1)} %m1_hbm.1, bf16[4,16,256]{2,1,0:T(8,128)(2,1)S(1)} %bitcast.1), custom_call_target="tpu_custom_call" | custom-call | flops 12999999488 | bytes 18000000 | tf_op jit(solution)/shard_map/pallas_call | solution.py:398
  92.4 0.8 copy.5
Async XLA Ops:
  0.0 0.8 copy-start
